TPU v7x, 32 devices: a whole 2x2x4 slice. The times are simulated.
32 devices in a mesh: tile: 16 (over z, y, x), mem: 2 (over core).
Axes of the slice: x: 2, y: 2, z: 4, core: 2. Of those that a mesh axis runs over, the one named last changes fastest.
Arguments:
- inc_fine: bfloat16 [6, 196608], P(None, 'tile'), may hold values from -8 to 11
- pair_owner: int32 [384, 4], P('tile'), may hold values from 0 to 15, all different within a row; in each aligned block of 24 rows (0 to 23, 24 to 47, ...) at most 12 rows name the same one
- pair_block: int32 [384, 4], P('tile'), may hold values from 0 to 95
- pair_count: int32 [384, 4], P('tile'), may hold values from 1 to 128
- pair_weight: bfloat16 [384, 4, 128, 128], P('tile'), may hold values from 0.049804688 to 1
- cell_area: float32 [49152], P('tile'), may hold values from 0.07 to 5.6
- prior: bfloat16 [6, 80, 49152], P(None, 'mem', 'tile'), may hold values from -6 to 6
- posterior: bfloat16 [6, 80, 49152], P(None, 'mem', 'tile'), may hold values from -4 to 4
Outputs:
- analysis: bfloat16 [6, 80, 49152], P(None, 'mem', 'tile')
Inputs may be any that keep to these rules, and one draw needn't show every extreme that they name: `pair_owner`: among the 24 rows of one device (aligned blocks) no owner is named more than 12 times, a bound that some block reaches; the 4 owners of a row differ.
All inputs are finite; a program needn't handle non-finite values.
Results may differ from a plain program's by a relative error of at most 0.0006.
Values may be sent and summed in bfloat16 or wider, within the bound.
A program may use at most 64 MiB of HBM per device.

v0:
```python
import jax
import jax.numpy as jnp
from jax import lax
from jax.sharding import PartitionSpec as P

relax_weight = 0.85
variance_eps = 1e-06


def remap_blocks(inc_fine, owner, block, count, weight, slot_cap, col_len):
    tile_count = lax.axis_size("tile")
    block_len = weight.shape[-1]
    channels = inc_fine.shape[0]
    coarse_rows = owner.shape[0]
    flat_owner = owner.reshape(-1)
    owner_match = (flat_owner[:, None] == jnp.arange(tile_count, dtype=jnp.int32)[None, :]).astype(
        jnp.int32
    )
    earlier = jnp.cumsum(owner_match, axis=0) - owner_match
    slot_index = jnp.sum(earlier * owner_match, axis=1)
    slot_target = flat_owner * slot_cap + slot_index
    wanted = jnp.zeros((tile_count * slot_cap,), jnp.int32).at[slot_target].set(block.reshape(-1))
    requested = lax.all_to_all(
        wanted.reshape(tile_count, slot_cap), "tile", split_axis=0, concat_axis=0, tiled=True
    )
    fine_rows = inc_fine.reshape(channels, -1, block_len)
    served = jnp.take(fine_rows, requested.reshape(-1), axis=1).reshape(
        channels, tile_count, slot_cap, col_len
    )
    live = jnp.arange(block_len, dtype=jnp.int32)[None, None, :] < count[:, :, None]
    masked = jnp.where(live[:, :, None, :], weight, jnp.zeros((), weight.dtype))
    weight_total = jnp.sum(masked.astype(jnp.float32), axis=(1, 3))
    piece = lax.all_to_all(served, "tile", split_axis=1, concat_axis=1, tiled=True)
    items = piece.shape[0]
    picked = jnp.take(piece.reshape(items, tile_count * slot_cap, col_len), slot_target, axis=1)
    picked = picked.reshape(items, coarse_rows, owner.shape[1], col_len)
    weighted = jnp.einsum("rpij,krpj->kri", masked, picked, preferred_element_type=jnp.float32)
    return (weighted.reshape(channels, coarse_rows * block_len), weight_total.reshape(-1))


def per_device(
    inc_fine, pair_owner, pair_block, pair_count, pair_weight, cell_area, prior, posterior
):
    tile_count = lax.axis_size("tile")
    mem_count = lax.axis_size("mem")
    block_rows = pair_owner.shape[0]
    pair_slots = pair_owner.shape[1]
    block_len = pair_weight.shape[-1]
    slot_cap = max(2, (2 * block_rows * pair_slots + tile_count - 1) // tile_count)
    weighted, total = remap_blocks(
        inc_fine, pair_owner, pair_block, pair_count, pair_weight, slot_cap, block_len
    )
    coarse = weighted / total[None, :]
    weighted_sum, area_total = lax.psum(
        (jnp.sum(coarse * cell_area[None, :], axis=1), jnp.sum(cell_area)), "tile"
    )
    increment = coarse - (weighted_sum / area_total)[:, None]
    members = prior.shape[1] * mem_count
    prior_wide = prior.astype(jnp.float32)
    post_wide = posterior.astype(jnp.float32)
    prior_sum, post_sum = lax.psum((jnp.sum(prior_wide, axis=1), jnp.sum(post_wide, axis=1)), "mem")
    prior_mean = prior_sum / members
    post_mean = post_sum / members
    prior_dev = prior_wide - prior_mean[:, None, :]
    post_dev = post_wide - post_mean[:, None, :]
    prior_square, post_square = lax.psum(
        (jnp.sum(prior_dev * prior_dev, axis=1), jnp.sum(post_dev * post_dev, axis=1)), "mem"
    )
    prior_var = prior_square / (members - 1)
    post_var = post_square / (members - 1)
    prior_spread = jnp.sqrt(prior_var + variance_eps)
    post_spread = jnp.sqrt(post_var + variance_eps)
    factor = 1.0 + relax_weight * (prior_spread - post_spread) / post_spread
    center = prior_mean + increment
    return (center[:, None, :] + factor[:, None, :] * post_dev).astype(jnp.bfloat16)


def solution(mesh):
    in_specs = (
        P(None, "tile"),
        P("tile", None),
        P("tile", None),
        P("tile", None),
        P("tile", None, None, None),
        P("tile"),
        P(None, "mem", "tile"),
        P(None, "mem", "tile"),
    )
    out_specs = P(None, "mem", "tile")
    return jax.shard_map(
        per_device, mesh=mesh, in_specs=in_specs, out_specs=out_specs, check_vma=False
    )
```

profile of v0, /device:TPU:0, one launch (start us, length us, event | category | flops | bytes accessed | tf_op | source)
XLA Modules:
  0.0 121.1 jit_solution(18386799340926691773)
XLA Ops:
  6.5 0.8 broadcast_multiply_fusion.2
  7.3 0.8 copy.28
  8.1 0.1 copy.31
  8.1 0.1 mul.56
  8.2 0.8 copy.32
  9.0 0.1 reshape.152
  9.1 0.1 reshape.125
  9.2 0.1 fusion.16
  9.3 0.1 reduce_window_sum.11
  9.4 0.2 select_reduce_fusion
  9.6 0.9 scatter_custom_fusion
  10.5 0.7 all_to_all.9
  11.2 8.3 %all-to-all-start = ((s32[16,1,12]{2,1,0:T(1,128)}), s32[16,1,12]{2,1,0:T(1,128)S(1)}, u32[]{:S(2)}, u32[]{:S(2)}) async-start(s32[16,1,12]{2,1,0:T(1,128)} %bitcast.2), calls=%async_computation | async-start | bytes 16384 | tf_op jit(solution)/shard_map/all_to_all | solution.py:23
  19.5 0.0 all-reduce.8.cloned.1.call-start
  19.6 2.5 %convert_reduce_fusion.2 = f32[6,3072]{1,0:T(8,128)} fusion(bf16[6,40,3072]{2,1,0:T(8,128)(2,1)} %param.14), kind=kLoop, calls=%fused_computation.7 | loop fusion | flops 1456128 | bytes 1548288 | tf_op jit(solution)/shard_map/reduce_sum | solution.py:61
  22.0 2.3 %convert_reduce_fusion.1 = f32[6,3072]{1,0:T(8,128)} fusion(bf16[6,40,3072]{2,1,0:T(8,128)(2,1)} %param.15), kind=kLoop, calls=%fused_computation.5 | loop fusion | flops 1456128 | bytes 1548288 | tf_op jit(solution)/shard_map/reduce_sum | solution.py:61
  24.4 0.0 all-reduce.8.cloned.1.call-update
  24.4 0.1 reduce_sum.78
  24.5 0.1 copy.29
  24.6 0.1 copy.38
  24.7 0.1 copy.30
  24.8 0.7 reduce_sum.82
  25.5 1.2 %all-to-all-done = s32[16,1,12]{2,1,0:T(1,128)S(1)} async-done(((s32[16,1,12]{2,1,0:T(1,128)}), s32[16,1,12]{2,1,0:T(1,128)S(1)}, u32[]{:S(2)}, u32[]{:S(2)}) %all-to-all-start) | async-done | bytes 800 | tf_op jit(solution)/shard_map/all_to_all | solution.py:23
  26.7 0.5 broadcast.126
  27.2 0.7 reduce.4
  27.9 0.1 reshape.129
  28.0 1.5 %gather_fusion = bf16[192,6,128]{2,1,0:T(8,128)(2,1)} fusion(bf16[6,96,128]{2,0,1:T(8,128)(2,1)S(1)} %bitcast.36, s32[1024]{0:T(1024)S(1)} %pad_clamp_fusion.1), kind=kCustom, calls=%fused_computation | custom fusion | bytes 590592 | tf_op jit(solution)/shard_map/jit(_take)/gather | solution.py:27
  29.5 1.1 copy_select_fusion
  30.6 0.8 copy.35
  31.4 5.7 %all-to-all-start.1 = ((bf16[6,16,12,128]{3,2,0,1:T(8,128)(2,1)}), bf16[6,16,12,128]{3,2,0,1:T(8,128)(2,1)}, u32[]{:S(2)}, u32[]{:S(2)}) async-start(bf16[6,16,12,128]{3,2,0,1:T(8,128)(2,1)} %copy.35), calls=%async_computation.1 | async-start | bytes 786432 | tf_op jit(solution)/shard_map/all_to_all | solution.py:33
  37.1 0.0 all-reduce.6.cloned.1.call-start
  37.2 0.1 iota_compare_fusion
  37.3 0.7 convert_reduce_fusion
  38.0 11.2 %all-to-all-done.1 = bf16[6,16,12,128]{3,2,0,1:T(8,128)(2,1)} async-done(((bf16[6,16,12,128]{3,2,0,1:T(8,128)(2,1)}), bf16[6,16,12,128]{3,2,0,1:T(8,128)(2,1)}, u32[]{:S(2)}, u32[]{:S(2)}) %all-to-all-start.1) | async-done | bytes 294944 | tf_op jit(solution)/shard_map/all_to_all | solution.py:33
  49.2 1.1 copy.41
  50.3 0.7 gather_fusion.1
  51.0 0.0 copy-start.1
  51.0 3.1 %fusion.15 = (f32[6]{0:T(128)S(1)}, f32[24,6,128,1]{2,1,3,0:T(8,128)S(1)}) fusion(f32[24,128]{1,0:T(8,128)S(1)} %bitcast.42, f32[24,128]{1,0:T(8,128)S(1)} %convert_reduce_fusion, bf16[24,4,128,128]{3,2,1,0:T(8,128)(2,1)} %param.12, pred[24,4,128]{2,1,0:T(4,128)(4,1)S(1)} %iota_compare_fusion, bf16[6,24,4,128]{3,0,2,1:T(8,128)(2,1)S(1)} %bitcast.39, ...), kind=kOutput, calls=%fused_computation.28 | convolution fusion | flops 20576250 | bytes 3403896 | tf_op jit(solution)/shard_map/rpij,krpj->kri/dot_general | solution.py:37
  54.1 39.3 %all-reduce = (f32[6]{0:T(128)S(1)}, f32[]{:T(128)}) all-reduce(f32[6]{0:T(128)S(1)} %get-tuple-element.13, f32[]{:T(128)} %reduce_sum.82), channel_id=1, replica_groups=mesh['tile'=16,'mem'=2] {'tile'}, use_global_device_ids=true, to_apply=%region_7.8 | all-reduce | flops 7 | bytes 56 | tf_op jit(solution)/shard_map/psum | solution.py:54
  93.4 0.6 broadcast_divide_fusion
  94.1 0.0 all-reduce.8.cloned.1.call-done
  94.1 1.0 fusion.12
  95.2 1.1 fusion.6
  96.3 1.1 fusion.2
  97.5 0.0 all-reduce.6.cloned.1.call-update
  97.5 14.2 %all-reduce.6.cloned.1.call-done = (f32[6,3072]{1,0:T(8,128)}, f32[6,3072]{1,0:T(8,128)}) async-done(((f32[6,3072]{1,0:T(8,128)}, f32[6,3072]{1,0:T(8,128)}), (f32[6,3072]{1,0:T(8,128)}, f32[6,3072]{1,0:T(8,128)})) %all-reduce.6.cloned.1.call-update) | async-done | bytes 147472 | tf_op jit(solution)/shard_map/psum | solution.py:66
  111.7 1.0 divide_add_fusion
  112.7 1.6 %fusion.4 = bf16[6,40,3072]{2,1,0:T(8,128)(2,1)} fusion(bf16[6,40,3072]{2,1,0:T(8,128)(2,1)S(1)} %copy-done.1, f32[6,3072]{1,0:T(8,128)S(1)} %divide_add_fusion, f32[6,3072]{1,0:T(8,128)S(1)} %get-tuple-element.15, f32[6,3072]{1,0:T(8,128)S(1)} %get-tuple-element.11), kind=kLoop, calls=%fused_computation.13 | loop fusion | flops 3686400 | bytes 3170304 | tf_op jit(solution)/shard_map/convert_element_type | solution.py:75
  (19 shorter events, 0.1 us)
Async XLA Ops:
  6.5 21.5 %copy-start = (bf16[6,12288]{1,0:T(8,128)(2,1)S(1)}, bf16[6,12288]{1,0:T(8,128)(2,1)}, u32[]{:S(2)}) copy-start(bf16[6,12288]{1,0:T(8,128)(2,1)} %param.8) | copy-start | bytes 442372
  6.5 18.0 %copy-start.4 = (s32[24,4]{0,1:T(4,128)S(1)}, s32[24,4]{0,1:T(4,128)}, u32[]{:S(2)}) copy-start(s32[24,4]{0,1:T(4,128)} %param.9) | copy-start | bytes 1156
  6.5 18.1 %copy-start.6 = (s32[24,4]{0,1:T(4,128)S(1)}, s32[24,4]{0,1:T(4,128)}, u32[]{:S(2)}) copy-start(s32[24,4]{0,1:T(4,128)} %param.11) | copy-start | bytes 1156
  6.5 18.3 %copy-start.5 = (f32[3072]{0:T(1024)S(1)}, f32[3072]{0:T(1024)}, u32[]{:S(2)}) copy-start(f32[3072]{0:T(1024)} %param.13) | copy-start | bytes 36868
  11.2 15.5 %all-to-all-start = ((s32[16,1,12]{2,1,0:T(1,128)}), s32[16,1,12]{2,1,0:T(1,128)S(1)}, u32[]{:S(2)}, u32[]{:S(2)}) async-start(s32[16,1,12]{2,1,0:T(1,128)} %bitcast.2), calls=%async_computation | async-start | bytes 16384 | tf_op jit(solution)/shard_map/all_to_all | solution.py:23
  19.5 17.7 %copy-start.3 = (bf16[24,4,128,128]{3,2,1,0:T(8,128)(2,1)S(1)}, bf16[24,4,128,128]{3,2,1,0:T(8,128)(2,1)}, u32[]{:S(2)}) copy-start(bf16[24,4,128,128]{3,2,1,0:T(8,128)(2,1)} %param.12) | copy-start | bytes 9437188
  19.5 74.6 %all-reduce.8.cloned.1.call-start = ((), (), s32[]{:S(2)}) async-start(), calls=%async_computation.3 | async-start | bytes 393216 | tf_op jit(solution)/shard_map/psum | solution.py:61
  31.4 17.8 %all-to-all-start.1 = ((bf16[6,16,12,128]{3,2,0,1:T(8,128)(2,1)}), bf16[6,16,12,128]{3,2,0,1:T(8,128)(2,1)}, u32[]{:S(2)}, u32[]{:S(2)}) async-start(bf16[6,16,12,128]{3,2,0,1:T(8,128)(2,1)} %copy.35), calls=%async_computation.1 | async-start | bytes 786432 | tf_op jit(solution)/shard_map/all_to_all | solution.py:33
  37.1 74.5 %all-reduce.6.cloned.1.call-start = ((), (), s32[]{:S(2)}) async-start(), calls=%async_computation.2 | async-start | bytes 393216 | tf_op jit(solution)/shard_map/psum | solution.py:66
  51.0 44.2 %copy-start.2 = (bf16[6,40,3072]{2,1,0:T(8,128)(2,1)S(1)}, bf16[6,40,3072]{2,1,0:T(8,128)(2,1)}, u32[]{:S(2)}) copy-start(bf16[6,40,3072]{2,1,0:T(8,128)(2,1)} %param.14) | copy-start | bytes 4423684
  51.0 45.3 %copy-start.1 = (bf16[6,40,3072]{2,1,0:T(8,128)(2,1)S(1)}, bf16[6,40,3072]{2,1,0:T(8,128)(2,1)}, u32[]{:S(2)}) copy-start(bf16[6,40,3072]{2,1,0:T(8,128)(2,1)} %param.15) | copy-start | bytes 4423684
Sparse Core Ops, SparseCore 0:
  24.5 19.4 all-reduce.7
  97.6 13.9 all-reduce.5
where the time goes:
time: 122 us; the launch traced here: 121 us
  blocking collectives  39.3 us (32%)
  waiting for transfers between devices  26.7 us (22%)
  other arithmetic  15.8 us (13%)
  starting transfers between devices  14.1 us (12%)
  between operations  13.6 us (11%)
  local copies, waits for them, and re-layouts  8.45 us (7%)
  matrix products  3.13 us (3%)
    psum x1, blocking collectives, per_device(): lax.psum((jnp.sum(coarse * cell_area[None, :], axis=1), jnp.sum(cell_area...  39.3 us
    psum x1, waiting for transfers between devices, per_device(): lax.psum((jnp.sum(prior_dev * prior_dev, axis=1), jnp.sum(post_dev * post...  14.2 us
    all_to_all x1, waiting for transfers between devices, remap_blocks(): lax.all_to_all(served, 'tile', split_axis=1, concat_axis=1, tiled=True)  11.2 us
    all_to_all x1, starting transfers between devices, remap_blocks(): lax.all_to_all(wanted.reshape(tile_count, slot_cap), 'tile', split_axis=0...  8.31 us
    all_to_all x1, starting transfers between devices, remap_blocks(): lax.all_to_all(served, 'tile', split_axis=1, concat_axis=1, tiled=True)  5.72 us
    dot_general x1, matrix products, remap_blocks(): jnp.einsum('rpij,krpj->kri', masked, picked, preferred_element_type=jnp.f...  3.13 us
    reduce_sum x1, other arithmetic, per_device(): jnp.sum(prior_wide, axis=1)  2.47 us
  transfers between devices with their start and end apart: 4, of which 3 were waited for; matrix products, arithmetic and copies ran while one was open for 14% of the time, Pallas kernels for 0%

commit v1 on v0

v1 whole, which is shorter than its diff:
```python
import functools

import jax
import jax.numpy as jnp
from jax import lax
from jax.experimental import pallas as pl
from jax.experimental.pallas import tpu as pltpu
from jax.sharding import PartitionSpec as P

relax_weight = 0.85
variance_eps = 1e-06
f32 = jnp.float32
bf16 = jnp.bfloat16
MESH = pl.DeviceIdType.MESH
LANES = 128
SUB = 8
ONES = 7


def round_up(n, k):
    return -(-n // k) * k


def kernel(
    tiles,
    mems,
    cap,
    inc_ref,
    owner_ref,
    block_ref,
    count_ref,
    area_ref,
    weight_hbm,
    prior_hbm,
    post_hbm,
    out_ref,
    weight,
    prior,
    post,
    tall,
    fine,
    before,
    square,
    hits,
    ask,
    asked,
    pick,
    served,
    got,
    spread,
    stats,
    coarse,
    level,
    local_sem,
    ask_send,
    ask_recv,
    data_send,
    data_recv,
    stat_send,
    stat_recv,
    coarse_send,
    coarse_recv,
    level_send,
    level_recv,
):
    channels = inc_ref.shape[0]
    rows, pairs = owner_ref.shape
    fblocks = inc_ref.shape[1] // LANES
    fine_pad = fine.shape[0]
    part = got.shape[1] // LANES
    slots = got.shape[0] // tiles
    row_pad = pick.shape[0] // pairs
    members, cells = prior.shape[1], prior.shape[2]
    devices = tiles * mems
    me = lax.axis_index("tile")
    core = lax.axis_index("mem")
    flat = me * mems + core
    first = jnp.minimum(core * part, channels - part)

    barrier = pltpu.get_barrier_semaphore()

    def greet(k, carry):
        other = lax.rem(flat + k, devices)
        pl.semaphore_signal(
            barrier, inc=1, device_id=(other // mems, lax.rem(other, mems)), device_id_type=MESH
        )
        return carry

    lax.fori_loop(1, devices, greet, 0)
    load_prior = pltpu.make_async_copy(prior_hbm, prior, local_sem.at[0])
    load_post = pltpu.make_async_copy(post_hbm, post, local_sem.at[1])
    load_weight = pltpu.make_async_copy(weight_hbm, weight, local_sem.at[2])
    load_prior.start()
    load_post.start()
    load_weight.start()

    lane = lax.broadcasted_iota(jnp.int32, (rows, LANES), 1)
    owner = owner_ref[...]
    block = block_ref[...]
    named = [owner[:, p : p + 1] == lane for p in range(pairs)]
    any_named = jnp.zeros((rows, LANES), f32)
    wanted = jnp.zeros((rows, LANES), f32)
    for p in range(pairs):
        any_named = any_named + jnp.where(named[p], 1.0, 0.0)
        wanted = wanted + jnp.where(named[p], (block[:, p : p + 1] + 1).astype(f32), 0.0)
    run = jnp.zeros((1, LANES), f32)
    for r in range(rows):
        before[r : r + 1, :] = run
        run = run + any_named[r : r + 1, :]
    earlier = before[...]
    square[...] = jnp.zeros_like(square)
    for s in range(cap):
        chosen = jnp.where((earlier == float(s)) & (any_named > 0.0), wanted, 0.0)
        square[s : s + 1, :] = jnp.sum(chosen, axis=0, keepdims=True)
    turned = jnp.transpose(square[...]) - 1.0
    for t in range(tiles):
        ask[t] = turned[t : t + 1, :]

    pl.semaphore_wait(barrier, devices - 1)

    def ask_copy(k, here):
        other = lax.rem(me + k, tiles)
        return pltpu.make_async_remote_copy(
            src_ref=ask.at[other],
            dst_ref=asked.at[here if here is not None else other],
            send_sem=ask_send.at[other],
            recv_sem=ask_recv.at[here if here is not None else other],
            device_id=(other, core),
            device_id_type=MESH,
        )

    def start_ask(k, carry):
        ask_copy(k, me).start()
        return carry

    lax.fori_loop(1, tiles, start_ask, 0)
    asked[pl.ds(me, 1)] = ask[pl.ds(me, 1)]

    for b in range(fblocks):
        tall[b * SUB : b * SUB + channels, :] = inc_ref[:, b * LANES : (b + 1) * LANES].astype(f32)
    fine[...] = jnp.zeros_like(fine)
    planes = [tall[pl.ds(c, fblocks, stride=SUB), :] for c in range(channels)]
    for k in range(part):
        value = planes[k]
        for c in range(1, channels):
            value = jnp.where(first + k == c, planes[c], value)
        fine[:fblocks, k * LANES : (k + 1) * LANES] = value.astype(bf16)

    wide = lax.broadcasted_iota(jnp.int32, (rows, tiles * slots), 1).astype(f32)
    pick[...] = jnp.zeros_like(pick)
    for p in range(pairs):
        slot = jnp.sum(jnp.where(named[p], earlier, 0.0), axis=1, keepdims=True)
        place = owner[:, p : p + 1].astype(f32) * float(slots) + slot
        pick[p * row_pad : p * row_pad + rows, :] = jnp.where(wide == place, 1.0, 0.0).astype(bf16)

    chunk = next(n for n in (512, 384, 256, 128) if cells % n == 0)
    sub = lax.broadcasted_iota(jnp.int32, (SUB, chunk), 0)

    def member_stats(ref, base):
        def body(j, carry):
            at = pl.ds(pl.multiple_of(j * chunk, chunk), chunk)
            sums = jnp.zeros((SUB, chunk), f32)
            squares = jnp.zeros((SUB, chunk), f32)
            for c in range(channels):
                values = ref[c, :, at].astype(f32)
                total = jnp.sum(values, axis=0, keepdims=True)
                dev = values - total * (1.0 / members)
                sq = jnp.sum(dev * dev, axis=0, keepdims=True)
                sums = jnp.where(sub == c, total, sums)
                squares = jnp.where(sub == c, sq, squares)
            stats[core, base : base + SUB, at] = sums
            stats[core, base + SUB : base + 2 * SUB, at] = squares
            return carry

        lax.fori_loop(0, cells // chunk, body, 0)

    load_prior.wait()
    member_stats(prior, 0)

    def wait_ask(k, carry):
        ask_copy(k, None).wait()
        return carry

    lax.fori_loop(1, tiles, wait_ask, 0)
    square[...] = jnp.zeros_like(square)
    for t in range(tiles):
        square[t : t + 1, :] = asked[t]
    turned = jnp.transpose(square[...])
    fine_lane = lax.broadcasted_iota(jnp.int32, (slots, fine_pad), 1).astype(f32)
    for t in range(tiles):
        hits[t * slots : (t + 1) * slots, :] = jnp.where(
            turned[:slots, t : t + 1] == fine_lane, 1.0, 0.0
        ).astype(bf16)
    served[...] = jnp.dot(hits[...], fine[...], preferred_element_type=f32).astype(bf16)

    def rows_of(t):
        return pl.ds(pl.multiple_of(t * slots, slots), slots)

    def data_copy(k, here):
        other = lax.rem(me + k, tiles)
        source = here if here is not None else other
        return pltpu.make_async_remote_copy(
            src_ref=served.at[rows_of(other)],
            dst_ref=got.at[rows_of(source)],
            send_sem=data_send.at[other],
            recv_sem=data_recv.at[source],
            device_id=(other, core),
            device_id_type=MESH,
        )

    def start_data(k, carry):
        data_copy(k, me).start()
        return carry

    lax.fori_loop(1, tiles, start_data, 0)
    got[rows_of(me), :] = served[rows_of(me), :]

    load_post.wait()
    member_stats(post, 2 * SUB)

    def core_copy(buffer, send, recv, k, here):
        other = lax.rem(core + k, mems)
        source = here if here is not None else other
        return pltpu.make_async_remote_copy(
            src_ref=buffer.at[core],
            dst_ref=buffer.at[source],
            send_sem=send.at[other],
            recv_sem=recv.at[source],
            device_id=(me, other),
            device_id_type=MESH,
        )

    for k in range(1, mems):
        core_copy(stats, stat_send, stat_recv, k, core).start()
    spread[...] = jnp.zeros_like(spread)
    for k in range(1, mems):
        core_copy(stats, stat_send, stat_recv, k, None).wait()
    everyone = members * mems
    for j in range(cells // chunk):
        at = slice(j * chunk, (j + 1) * chunk)

        def combined(base):
            sums = [stats[m, base : base + SUB, at] for m in range(mems)]
            mean = functools.reduce(jnp.add, sums) * (1.0 / everyone)
            total = functools.reduce(
                jnp.add, [stats[m, base + SUB : base + 2 * SUB, at] for m in range(mems)]
            )
            for s in sums:
                off = s * (1.0 / members) - mean
                total = total + members * (off * off)
            return mean, jnp.sqrt(total * (1.0 / (everyone - 1)) + variance_eps)

        prior_mean, prior_spread = combined(0)
        post_mean, post_spread = combined(2 * SUB)
        out_ref[0, :, at] = prior_mean
        out_ref[1, :, at] = 1.0 + relax_weight * (prior_spread - post_spread) / post_spread
        out_ref[2, :, at] = post_mean

    load_weight.wait()

    def wait_data(k, carry):
        data_copy(k, None).wait()
        return carry

    lax.fori_loop(1, tiles, wait_data, 0)
    picked = jnp.dot(pick[...], got[...], preferred_element_type=f32)
    count = count_ref[...]
    for p in range(pairs):
        live = lane < count[:, p : p + 1]
        for c in range(channels):
            value = jnp.zeros((rows, LANES), f32)
            for k in range(part):
                mine = picked[p * row_pad : p * row_pad + rows, k * LANES : (k + 1) * LANES]
                value = jnp.where((first + k == c) & (core * part < channels), mine, value)
            spread[p, pl.ds(c, rows, stride=SUB), :] = jnp.where(live, value, 0.0)
        spread[p, pl.ds(ONES, rows, stride=SUB), :] = jnp.where(live, 1.0, 0.0)

    group = next(n for n in (4, 3, 2, 1) if rows % n == 0)

    def remap(g, sums):
        for i in range(group):
            r = g * group + i
            here = pl.ds(pl.multiple_of(r * SUB, SUB), SUB)
            left = jnp.concatenate([spread[p, here, :] for p in range(pairs)], axis=1).astype(bf16)
            right = jnp.concatenate([weight[r, p] for p in range(pairs)], axis=1)
            product = lax.dot_general(
                left, right, (((1,), (1,)), ((), ())), preferred_element_type=f32
            )
            value = product / product[ONES : ONES + 1, :]
            coarse[core, :, pl.ds(pl.multiple_of(r * LANES, LANES), LANES)] = value
            sums = sums + value * area_ref[pl.ds(r, 1), :]
        return sums

    sums = lax.fori_loop(0, rows // group, remap, jnp.zeros((SUB, LANES), f32))

    for k in range(1, mems):
        core_copy(coarse, coarse_send, coarse_recv, k, core).start()
    eye = lax.broadcasted_iota(jnp.int32, (SUB, LANES), 0) == lax.broadcasted_iota(
        jnp.int32, (SUB, LANES), 1
    )
    total = jnp.sum(sums, axis=1, keepdims=True)
    level[pl.ds(flat, 1)] = jnp.sum(jnp.where(eye, total, 0.0), axis=0, keepdims=True)[None]

    def level_copy(k, here):
        other = lax.rem(flat + k, devices)
        source = here if here is not None else other
        return pltpu.make_async_remote_copy(
            src_ref=level.at[flat],
            dst_ref=level.at[source],
            send_sem=level_send.at[other],
            recv_sem=level_recv.at[source],
            device_id=(other // mems, lax.rem(other, mems)),
            device_id_type=MESH,
        )

    def start_level(k, carry):
        level_copy(k, flat).start()
        return carry

    def wait_level(k, carry):
        level_copy(k, None).wait()
        return carry

    lax.fori_loop(1, devices, start_level, 0)
    for k in range(1, mems):
        core_copy(coarse, coarse_send, coarse_recv, k, None).wait()
    lax.fori_loop(1, devices, wait_level, 0)
    row = level[0]
    for d in range(1, devices):
        row = row + level[d]
    weighted = jnp.sum(jnp.where(eye, row, 0.0), axis=1, keepdims=True)
    area = weighted[ONES : ONES + 1, :] * (1.0 / mems)
    mean = weighted / area
    for j in range(cells // chunk):
        at = slice(j * chunk, (j + 1) * chunk)
        value = functools.reduce(jnp.add, [coarse[m, :, at] for m in range(mems)])
        out_ref[0, :, at] = out_ref[0, :, at] + (value - mean)


def per_device(
    inc_fine, pair_owner, pair_block, pair_count, pair_weight, cell_area, prior, posterior
):
    tiles = lax.axis_size("tile")
    mems = lax.axis_size("mem")
    channels, fine_cells = inc_fine.shape
    rows, pairs = pair_owner.shape
    cells = prior.shape[2]
    fblocks = fine_cells // LANES
    cap = max(2, (2 * rows * pairs + tiles - 1) // tiles)
    cap = min(cap, rows)
    slots = round_up(cap, 16)
    part = -(-channels // mems)
    fine_pad = round_up(fblocks, LANES)
    row_pad = round_up(rows, 16)
    devices = tiles * mems
    vmem = pl.BlockSpec(memory_space=pltpu.VMEM)
    hbm = pl.BlockSpec(memory_space=pl.ANY)
    dma = pltpu.SemaphoreType.DMA
    small = pl.pallas_call(
        functools.partial(kernel, tiles, mems, cap),
        out_shape=jax.ShapeDtypeStruct((3, SUB, cells), f32),
        in_specs=[vmem] * 5 + [hbm] * 3,
        out_specs=vmem,
        scratch_shapes=[
            pltpu.VMEM(pair_weight.shape, bf16),
            pltpu.VMEM(prior.shape, bf16),
            pltpu.VMEM(posterior.shape, bf16),
            pltpu.VMEM((fblocks * SUB, LANES), f32),
            pltpu.VMEM((fine_pad, part * LANES), bf16),
            pltpu.VMEM((rows, LANES), f32),
            pltpu.VMEM((LANES, LANES), f32),
            pltpu.VMEM((tiles * slots, fine_pad), bf16),
            pltpu.VMEM((tiles, 1, LANES), f32),
            pltpu.VMEM((tiles, 1, LANES), f32),
            pltpu.VMEM((pairs * row_pad, tiles * slots), bf16),
            pltpu.VMEM((tiles * slots, part * LANES), bf16),
            pltpu.VMEM((tiles * slots, part * LANES), bf16),
            pltpu.VMEM((pairs, rows * SUB, LANES), f32),
            pltpu.VMEM((mems, 4 * SUB, cells), f32),
            pltpu.VMEM((mems, SUB, cells), f32),
            pltpu.VMEM((devices, 1, LANES), f32),
            dma((3,)),
            dma((tiles,)),
            dma((tiles,)),
            dma((tiles,)),
            dma((tiles,)),
            dma((mems,)),
            dma((mems,)),
            dma((mems,)),
            dma((mems,)),
            dma((devices,)),
            dma((devices,)),
        ],
        compiler_params=pltpu.CompilerParams(
            collective_id=0, has_side_effects=True, vmem_limit_bytes=48 * 1024 * 1024
        ),
        name="remap_and_spread",
    )(
        inc_fine,
        pair_owner,
        pair_block,
        pair_count,
        cell_area.reshape(rows, -1),
        pair_weight,
        prior,
        posterior,
    )
    center, factor, post_mean = (small[i, :channels, None, :] for i in range(3))
    return (center + factor * (posterior.astype(f32) - post_mean)).astype(bf16)


def solution(mesh):
    in_specs = (
        P(None, "tile"),
        P("tile", None),
        P("tile", None),
        P("tile", None),
        P("tile", None, None, None),
        P("tile"),
        P(None, "mem", "tile"),
        P(None, "mem", "tile"),
    )
    out_specs = P(None, "mem", "tile")
    return jax.shard_map(
        per_device, mesh=mesh, in_specs=in_specs, out_specs=out_specs, check_vma=False
    )
```

time: 122 us -> 32.9 us (0.27)
  blocking collectives: 39.3 us -> 0 us
  waiting for transfers between devices: 26.7 us -> 0 us
  Pallas kernels: 0 us -> 24.3 us
  other arithmetic: 15.8 us -> 1.58 us
  starting transfers between devices: 14.1 us -> 0 us
  between operations: 13.6 us -> 0.02 us
  matrix products: 3.13 us -> 0 us
  local copies, waits for them, and re-layouts: 8.45 us -> 6.68 us
    psum x1 -> x0, blocking collectives: 39.3 us -> none  [per_device(): lax.psum((jnp.sum(coarse * cell_area[None, :], axis=1), jnp.sum(cell_area...]
    pallas_call x0 -> x1, Pallas kernels: none -> 24.3 us  [per_device(): pl.pallas_call(functools.partial(kernel, tiles, mems, cap), out_shape=jax...]
    psum x2 -> x0, waiting for transfers between devices: 14.2 us -> none  [the longest x1 14.2 us: per_device(): lax.psum((jnp.sum(prior_dev * prior_dev, axis=1), jnp.sum(post_dev * post...]
    all_to_all x2 -> x0, starting transfers between devices: 14 us -> none  [the longest x1 8.31 us: remap_blocks(): lax.all_to_all(wanted.reshape(tile_count, slot_cap), 'tile', split_axis=0...]
    all_to_all x2 -> x0, waiting for transfers between devices: 12.4 us -> none  [the longest x1 11.2 us: remap_blocks(): lax.all_to_all(served, 'tile', split_axis=1, concat_axis=1, tiled=True)]
    reduce_sum x7 -> x0, other arithmetic: 8.66 us -> none  [the longest x1 2.47 us: per_device(): jnp.sum(prior_wide, axis=1)]
    unnamed x17 -> x11, local copies, waits for them, and re-layouts: 1.64 us -> 6.66 us
    dot_general x1 -> x0, matrix products: 3.13 us -> none  [remap_blocks(): jnp.einsum('rpij,krpj->kri', masked, picked, preferred_element_type=jnp.f...]
  transfers between devices with their start and end apart: 4 -> 0, of which waited for: 3 -> 0; matrix products, arithmetic and copies ran while one was open for 14% -> 0% of each run, Pallas kernels for 0% -> 0%
where the time goes in v1:
time: 32.9 us; the launch traced here: 32.6 us
  Pallas kernels  24.3 us (74%)
  local copies, waits for them, and re-layouts  6.68 us (20%)
  other arithmetic  1.58 us (5%)
    pallas_call x1, Pallas kernels, per_device(): pl.pallas_call(functools.partial(kernel, tiles, mems, cap), out_shape=jax...  24.3 us
    unnamed x11, local copies, waits for them, and re-layouts  6.66 us
    convert_element_type x1, other arithmetic, per_device(): return (center + factor * (posterior.astype(f32) - post_mean)).astype(bf16)  1.58 us

profile of v1, /device:TPU:0, one launch (start us, length us, event | category | flops | bytes accessed | tf_op | source)
XLA Modules:
  0.0 32.6 jit_solution(12401733455572331670)
XLA Ops:
  0.0 0.8 %copy.9.owner_ref = s32[24,4]{1,0:T(8,128)S(1)} copy(s32[24,4]{0,1:T(4,128)} %param.9) | data formatting | bytes 768 | tf_op args[1]
  0.8 0.8 %copy.10.block_ref = s32[24,4]{1,0:T(8,128)S(1)} copy(s32[24,4]{0,1:T(4,128)} %param.10) | data formatting | bytes 768 | tf_op args[2]
  1.5 0.8 %copy.11.count_ref = s32[24,4]{1,0:T(8,128)S(1)} copy(s32[24,4]{0,1:T(4,128)} %param.11) | data formatting | bytes 768 | tf_op args[3]
  2.3 0.0 copy-start
  2.3 1.4 %copy-done = bf16[6,40,3072]{2,1,0:T(8,128)(2,1)S(1)} copy-done((bf16[6,40,3072]{2,1,0:T(8,128)(2,1)S(1)}, bf16[6,40,3072]{2,1,0:T(8,128)(2,1)}, u32[]{:S(2)}) %copy-start) | copy-done | bytes 1474584
  3.7 0.0 copy-start.1
  3.7 1.4 %copy-done.1 = bf16[6,40,3072]{2,1,0:T(8,128)(2,1)S(1)} copy-done((bf16[6,40,3072]{2,1,0:T(8,128)(2,1)S(1)}, bf16[6,40,3072]{2,1,0:T(8,128)(2,1)}, u32[]{:S(2)}) %copy-start.1) | copy-done | bytes 1474584
  5.0 0.0 copy-start.2
  5.0 0.9 %copy-done.2 = bf16[6,12288]{1,0:T(8,128)(2,1)S(1)} copy-done((bf16[6,12288]{1,0:T(8,128)(2,1)S(1)}, bf16[6,12288]{1,0:T(8,128)(2,1)}, u32[]{:S(2)}) %copy-start.2) | copy-done | bytes 147480
  6.0 0.0 copy-start.3
  6.0 0.7 %copy-done.3 = f32[3072]{0:T(1024)S(1)} copy-done((f32[3072]{0:T(1024)S(1)}, f32[3072]{0:T(1024)}, u32[]{:S(2)}) %copy-start.3) | copy-done | bytes 12312
  6.7 24.3 %remap_and_spread.1 = f32[3,8,3072]{2,1,0:T(8,128)S(1)} custom-call(bf16[6,12288]{1,0:T(8,128)(2,1)S(1)} %copy-done.2, s32[24,4]{1,0:T(8,128)S(1)} %copy.9.owner_ref, s32[24,4]{1,0:T(8,128)S(1)} %copy.10.block_ref, s32[24,4]{1,0:T(8,128)S(1)} %copy.11.count_ref, f32[24,128]{1,0:T(8,128)S(1)} %bitcast.7, bf16[24,4,128,128]{3,2,1,0:T(8,128)(2,1)} %weight_hbm.1, ...), custom_call_target="tpu_custom_call" | custom-call | tf_op jit(solution)/shard_map/remap_and_spread/pallas_call | solution.py:359
  31.0 1.6 %add_convert_fusion = bf16[6,40,3072]{2,1,0:T(8,128)(2,1)} fusion(bf16[6,40,3072]{2,1,0:T(8,128)(2,1)S(1)} %copy-done, f32[6,3072]{1,0:T(8,128)S(1)} %get-tuple-element.6, f32[6,3072]{1,0:T(8,128)S(1)} %get-tuple-element.7, f32[6,3072]{1,0:T(8,128)S(1)} %get-tuple-element.5), kind=kLoop, calls=%fused_computation | loop fusion | flops 3686400 | bytes 3170304 | tf_op jit(solution)/shard_map/convert_element_type | solution.py:409
  (1 shorter events, 0.0 us)
Async XLA Ops:
  2.3 1.4 %copy-start = (bf16[6,40,3072]{2,1,0:T(8,128)(2,1)S(1)}, bf16[6,40,3072]{2,1,0:T(8,128)(2,1)}, u32[]{:S(2)}) copy-start(bf16[6,40,3072]{2,1,0:T(8,128)(2,1)} %post_hbm.1) | copy-start | bytes 4423684
  3.7 1.4 %copy-start.1 = (bf16[6,40,3072]{2,1,0:T(8,128)(2,1)S(1)}, bf16[6,40,3072]{2,1,0:T(8,128)(2,1)}, u32[]{:S(2)}) copy-start(bf16[6,40,3072]{2,1,0:T(8,128)(2,1)} %prior_hbm.1) | copy-start | bytes 4423684
  5.0 0.9 %copy-start.2 = (bf16[6,12288]{1,0:T(8,128)(2,1)S(1)}, bf16[6,12288]{1,0:T(8,128)(2,1)}, u32[]{:S(2)}) copy-start(bf16[6,12288]{1,0:T(8,128)(2,1)} %inc_ref.1) | copy-start | bytes 442372
  6.0 0.7 %copy-start.3 = (f32[3072]{0:T(1024)S(1)}, f32[3072]{0:T(1024)}, u32[]{:S(2)}) copy-start(f32[3072]{0:T(1024)} %param.13) | copy-start | bytes 36868

commit v2 on v1

--- a/solution.py
+++ b/solution.py
@@ -25,15 +25,18 @@
     tiles,
     mems,
     cap,
-    inc_ref,
-    owner_ref,
-    block_ref,
-    count_ref,
-    area_ref,
+    inc_hbm,
+    owner_hbm,
+    block_hbm,
+    count_hbm,
+    area_hbm,
     weight_hbm,
     prior_hbm,
     post_hbm,
     out_ref,
+    inc_ref,
+    index,
+    area_ref,
     weight,
     prior,
     post,
@@ -64,7 +67,7 @@
     level_recv,
 ):
     channels = inc_ref.shape[0]
-    rows, pairs = owner_ref.shape
+    pairs, rows = owner_hbm.shape
     fblocks = inc_ref.shape[1] // LANES
     fine_pad = fine.shape[0]
     part = got.shape[1] // LANES
@@ -77,6 +80,24 @@
     flat = me * mems + core
     first = jnp.minimum(core * part, channels - part)
 
+    loads = [
+        pltpu.make_async_copy(source, target, local_sem.at[i])
+        for i, (source, target) in enumerate(
+            [
+                (owner_hbm, index.at[0]),
+                (block_hbm, index.at[1]),
+                (count_hbm, index.at[2]),
+                (inc_hbm, inc_ref),
+                (prior_hbm, prior),
+                (weight_hbm, weight),
+                (post_hbm, post),
+                (area_hbm, area_ref),
+            ]
+        )
+    ]
+    for load in loads[:4]:
+        load.start()
+
     barrier = pltpu.get_barrier_semaphore()
 
     def greet(k, carry):
@@ -87,22 +108,23 @@
         return carry
 
     lax.fori_loop(1, devices, greet, 0)
-    load_prior = pltpu.make_async_copy(prior_hbm, prior, local_sem.at[0])
-    load_post = pltpu.make_async_copy(post_hbm, post, local_sem.at[1])
-    load_weight = pltpu.make_async_copy(weight_hbm, weight, local_sem.at[2])
-    load_prior.start()
-    load_post.start()
-    load_weight.start()
-
-    lane = lax.broadcasted_iota(jnp.int32, (rows, LANES), 1)
-    owner = owner_ref[...]
-    block = block_ref[...]
+    for load in loads[4:]:
+        load.start()
+
+    lane = lax.broadcasted_iota(jnp.int32, (rows, LANES), 1).astype(f32)
+    square[...] = jnp.zeros_like(square)
+    for load in loads[:3]:
+        load.wait()
+    for i in range(3):
+        square[i * SUB : i * SUB + pairs, :rows] = index[i].astype(f32)
+    turned = jnp.transpose(square[...])[:rows]
+    owner, block, count = (turned[:, i * SUB : i * SUB + pairs] for i in range(3))
     named = [owner[:, p : p + 1] == lane for p in range(pairs)]
     any_named = jnp.zeros((rows, LANES), f32)
     wanted = jnp.zeros((rows, LANES), f32)
     for p in range(pairs):
         any_named = any_named + jnp.where(named[p], 1.0, 0.0)
-        wanted = wanted + jnp.where(named[p], (block[:, p : p + 1] + 1).astype(f32), 0.0)
+        wanted = wanted + jnp.where(named[p], block[:, p : p + 1] + 1.0, 0.0)
     run = jnp.zeros((1, LANES), f32)
     for r in range(rows):
         before[r : r + 1, :] = run
@@ -116,26 +138,7 @@
     for t in range(tiles):
         ask[t] = turned[t : t + 1, :]
 
-    pl.semaphore_wait(barrier, devices - 1)
-
-    def ask_copy(k, here):
-        other = lax.rem(me + k, tiles)
-        return pltpu.make_async_remote_copy(
-            src_ref=ask.at[other],
-            dst_ref=asked.at[here if here is not None else other],
-            send_sem=ask_send.at[other],
-            recv_sem=ask_recv.at[here if here is not None else other],
-            device_id=(other, core),
-            device_id_type=MESH,
-        )
-
-    def start_ask(k, carry):
-        ask_copy(k, me).start()
-        return carry
-
-    lax.fori_loop(1, tiles, start_ask, 0)
-    asked[pl.ds(me, 1)] = ask[pl.ds(me, 1)]
-
+    loads[3].wait()
     for b in range(fblocks):
         tall[b * SUB : b * SUB + channels, :] = inc_ref[:, b * LANES : (b + 1) * LANES].astype(f32)
     fine[...] = jnp.zeros_like(fine)
@@ -150,8 +153,30 @@
     pick[...] = jnp.zeros_like(pick)
     for p in range(pairs):
         slot = jnp.sum(jnp.where(named[p], earlier, 0.0), axis=1, keepdims=True)
-        place = owner[:, p : p + 1].astype(f32) * float(slots) + slot
+        place = owner[:, p : p + 1] * float(slots) + slot
         pick[p * row_pad : p * row_pad + rows, :] = jnp.where(wide == place, 1.0, 0.0).astype(bf16)
+
+    live = [lane < count[:, p : p + 1] for p in range(pairs)]
+    spread[...] = jnp.zeros_like(spread)
+    for p in range(pairs):
+        spread[p, pl.ds(ONES, rows, stride=SUB), :] = jnp.where(live[p], 1.0, 0.0)
+
+    pl.semaphore_wait(barrier, devices - 1)
+
+    def start_ask(k, carry):
+        other = lax.rem(me + k, tiles)
+        pltpu.make_async_remote_copy(
+            src_ref=ask.at[other],
+            dst_ref=asked.at[me],
+            send_sem=ask_send,
+            recv_sem=ask_recv,
+            device_id=(other, core),
+            device_id_type=MESH,
+        ).start()
+        return carry
+
+    lax.fori_loop(1, tiles, start_ask, 0)
+    asked[pl.ds(me, 1)] = ask[pl.ds(me, 1)]
 
     chunk = next(n for n in (512, 384, 256, 128) if cells % n == 0)
     sub = lax.broadcasted_iota(jnp.int32, (SUB, chunk), 0)
@@ -174,14 +199,13 @@
 
         lax.fori_loop(0, cells // chunk, body, 0)
 
-    load_prior.wait()
+    loads[4].wait()
     member_stats(prior, 0)
 
-    def wait_ask(k, carry):
-        ask_copy(k, None).wait()
-        return carry
-
-    lax.fori_loop(1, tiles, wait_ask, 0)
+    def wait_all(buffer, sem):
+        pltpu.make_async_copy(buffer, buffer, sem).wait()
+
+    wait_all(asked.at[: tiles - 1], ask_recv)
     square[...] = jnp.zeros_like(square)
     for t in range(tiles):
         square[t : t + 1, :] = asked[t]
@@ -196,26 +220,22 @@
     def rows_of(t):
         return pl.ds(pl.multiple_of(t * slots, slots), slots)
 
-    def data_copy(k, here):
+    def start_data(k, carry):
         other = lax.rem(me + k, tiles)
-        source = here if here is not None else other
-        return pltpu.make_async_remote_copy(
+        pltpu.make_async_remote_copy(
             src_ref=served.at[rows_of(other)],
-            dst_ref=got.at[rows_of(source)],
-            send_sem=data_send.at[other],
-            recv_sem=data_recv.at[source],
+            dst_ref=got.at[rows_of(me)],
+            send_sem=data_send,
+            recv_sem=data_recv,
             device_id=(other, core),
             device_id_type=MESH,
-        )
-
-    def start_data(k, carry):
-        data_copy(k, me).start()
+        ).start()
         return carry
 
     lax.fori_loop(1, tiles, start_data, 0)
     got[rows_of(me), :] = served[rows_of(me), :]
 
-    load_post.wait()
+    loads[6].wait()
     member_stats(post, 2 * SUB)
 
     def core_copy(buffer, send, recv, k, here):
@@ -232,7 +252,6 @@
 
     for k in range(1, mems):
         core_copy(stats, stat_send, stat_recv, k, core).start()
-    spread[...] = jnp.zeros_like(spread)
     for k in range(1, mems):
         core_copy(stats, stat_send, stat_recv, k, None).wait()
     everyone = members * mems
@@ -256,26 +275,20 @@
         out_ref[1, :, at] = 1.0 + relax_weight * (prior_spread - post_spread) / post_spread
         out_ref[2, :, at] = post_mean
 
-    load_weight.wait()
-
-    def wait_data(k, carry):
-        data_copy(k, None).wait()
-        return carry
-
-    lax.fori_loop(1, tiles, wait_data, 0)
+    loads[5].wait()
+    loads[7].wait()
+
+    wait_all(got.at[: (tiles - 1) * slots], data_recv)
     picked = jnp.dot(pick[...], got[...], preferred_element_type=f32)
-    count = count_ref[...]
     for p in range(pairs):
-        live = lane < count[:, p : p + 1]
         for c in range(channels):
             value = jnp.zeros((rows, LANES), f32)
             for k in range(part):
                 mine = picked[p * row_pad : p * row_pad + rows, k * LANES : (k + 1) * LANES]
                 value = jnp.where((first + k == c) & (core * part < channels), mine, value)
-            spread[p, pl.ds(c, rows, stride=SUB), :] = jnp.where(live, value, 0.0)
-        spread[p, pl.ds(ONES, rows, stride=SUB), :] = jnp.where(live, 1.0, 0.0)
-
-    group = next(n for n in (4, 3, 2, 1) if rows % n == 0)
+            spread[p, pl.ds(c, rows, stride=SUB), :] = jnp.where(live[p], value, 0.0)
+
+    group = next(n for n in (12, 8, 4, 3, 2, 1) if rows % n == 0)
 
     def remap(g, sums):
         for i in range(group):
@@ -301,30 +314,22 @@
     total = jnp.sum(sums, axis=1, keepdims=True)
     level[pl.ds(flat, 1)] = jnp.sum(jnp.where(eye, total, 0.0), axis=0, keepdims=True)[None]
 
-    def level_copy(k, here):
+    def start_level(k, carry):
         other = lax.rem(flat + k, devices)
-        source = here if here is not None else other
-        return pltpu.make_async_remote_copy(
+        pltpu.make_async_remote_copy(
             src_ref=level.at[flat],
-            dst_ref=level.at[source],
-            send_sem=level_send.at[other],
-            recv_sem=level_recv.at[source],
+            dst_ref=level.at[flat],
+            send_sem=level_send,
+            recv_sem=level_recv,
             device_id=(other // mems, lax.rem(other, mems)),
             device_id_type=MESH,
-        )
-
-    def start_level(k, carry):
-        level_copy(k, flat).start()
-        return carry
-
-    def wait_level(k, carry):
-        level_copy(k, None).wait()
+        ).start()
         return carry
 
     lax.fori_loop(1, devices, start_level, 0)
     for k in range(1, mems):
         core_copy(coarse, coarse_send, coarse_recv, k, None).wait()
-    lax.fori_loop(1, devices, wait_level, 0)
+    wait_all(level.at[: devices - 1], level_recv)
     row = level[0]
     for d in range(1, devices):
         row = row + level[d]
@@ -335,6 +340,9 @@
         at = slice(j * chunk, (j + 1) * chunk)
         value = functools.reduce(jnp.add, [coarse[m, :, at] for m in range(mems)])
         out_ref[0, :, at] = out_ref[0, :, at] + (value - mean)
+    wait_all(asked.at[: tiles - 1], ask_send)
+    wait_all(got.at[: (tiles - 1) * slots], data_send)
+    wait_all(level.at[: devices - 1], level_send)
 
 
 def per_device(
@@ -354,14 +362,17 @@
     row_pad = round_up(rows, 16)
     devices = tiles * mems
     vmem = pl.BlockSpec(memory_space=pltpu.VMEM)
-    hbm = pl.BlockSpec(memory_space=pl.ANY)
+    hbm = pl.BlockSpec(memory_space=pltpu.HBM)
     dma = pltpu.SemaphoreType.DMA
     small = pl.pallas_call(
         functools.partial(kernel, tiles, mems, cap),
-        out_shape=jax.ShapeDtypeStruct((3, SUB, cells), f32),
-        in_specs=[vmem] * 5 + [hbm] * 3,
+        out_shape=pltpu.VMEM((3, SUB, cells), f32),
+        in_specs=[hbm] * 8,
         out_specs=vmem,
         scratch_shapes=[
+            pltpu.VMEM(inc_fine.shape, bf16),
+            pltpu.VMEM((3, pairs, rows), jnp.int32),
+            pltpu.VMEM((rows, LANES), f32),
             pltpu.VMEM(pair_weight.shape, bf16),
             pltpu.VMEM(prior.shape, bf16),
             pltpu.VMEM(posterior.shape, bf16),
@@ -379,27 +390,27 @@
             pltpu.VMEM((mems, 4 * SUB, cells), f32),
             pltpu.VMEM((mems, SUB, cells), f32),
             pltpu.VMEM((devices, 1, LANES), f32),
-            dma((3,)),
-            dma((tiles,)),
-            dma((tiles,)),
-            dma((tiles,)),
-            dma((tiles,)),
+            dma((8,)),
+            dma,
+            dma,
+            dma,
+            dma,
             dma((mems,)),
             dma((mems,)),
             dma((mems,)),
             dma((mems,)),
-            dma((devices,)),
-            dma((devices,)),
+            dma,
+            dma,
         ],
         compiler_params=pltpu.CompilerParams(
-            collective_id=0, has_side_effects=True, vmem_limit_bytes=48 * 1024 * 1024
+            collective_id=0, has_side_effects=True, vmem_limit_bytes=56 * 1024 * 1024
         ),
         name="remap_and_spread",
     )(
         inc_fine,
-        pair_owner,
-        pair_block,
-        pair_count,
+        pair_owner.T,
+        pair_block.T,
+        pair_count.T,
         cell_area.reshape(rows, -1),
         pair_weight,
         prior,

time: 32.9 us -> 24.6 us (0.75)
  local copies, waits for them, and re-layouts: 6.68 us -> 0.03 us
  Pallas kernels: 24.3 us -> 22.8 us
    unnamed x11 -> x2, local copies, waits for them, and re-layouts: 6.66 us -> 0.01 us
    pallas_call x1, Pallas kernels: 24.3 us -> 22.8 us  [per_device(): pl.pallas_call(functools.partial(kernel, tiles, mems, cap), out_shape=plt...]
where the time goes in v2:
time: 24.6 us; the launch traced here: 24.4 us
  Pallas kernels  22.8 us (93%)
  other arithmetic  1.58 us (6%)
    pallas_call x1, Pallas kernels, per_device(): pl.pallas_call(functools.partial(kernel, tiles, mems, cap), out_shape=plt...  22.8 us
    convert_element_type x1, other arithmetic, per_device(): return (center + factor * (posterior.astype(f32) - post_mean)).astype(bf16)  1.58 us

profile of v2, /device:TPU:0, one launch (start us, length us, event | category | flops | bytes accessed | tf_op | source)
XLA Modules:
  0.0 24.4 jit_solution(11830460611150249647)
XLA Ops:
  0.0 0.0 copy-start
  0.0 22.8 %remap_and_spread.1 = f32[3,8,3072]{2,1,0:T(8,128)S(1)} custom-call(bf16[6,12288]{1,0:T(8,128)(2,1)} %inc_hbm.1, s32[4,24]{1,0:T(4,128)} %bitcast.11, s32[4,24]{1,0:T(4,128)} %bitcast.12, s32[4,24]{1,0:T(4,128)} %bitcast.13, f32[24,128]{1,0:T(8,128)} %bitcast.10, bf16[24,4,128,128]{3,2,1,0:T(8,128)(2,1)} %weight_hbm.1, bf16[6,40,3072]{2,1,0:T(8,128)(2,1)} %prior_hbm.1, ...), custom_call_target="tpu_custom_call" | custom-call | tf_op jit(solution)/shard_map/remap_and_spread/pallas_call | solution.py:367
  22.8 0.0 copy-done
  22.9 1.6 %add_convert_fusion = bf16[6,40,3072]{2,1,0:T(8,128)(2,1)} fusion(bf16[6,40,3072]{2,1,0:T(8,128)(2,1)S(1)} %copy-done, f32[6,3072]{1,0:T(8,128)S(1)} %get-tuple-element.6, f32[6,3072]{1,0:T(8,128)S(1)} %get-tuple-element.7, f32[6,3072]{1,0:T(8,128)S(1)} %get-tuple-element.5), kind=kLoop, calls=%fused_computation | loop fusion | flops 3686400 | bytes 3170304 | tf_op jit(solution)/shard_map/convert_element_type | solution.py:420
  (1 shorter events, 0.0 us)
Async XLA Ops:
  0.0 22.9 %copy-start = (bf16[6,40,3072]{2,1,0:T(8,128)(2,1)S(1)}, bf16[6,40,3072]{2,1,0:T(8,128)(2,1)}, u32[]{:S(2)}) copy-start(bf16[6,40,3072]{2,1,0:T(8,128)(2,1)} %post_hbm.1) | copy-start | bytes 4423684

commit v3 on v2

--- a/solution.py
+++ b/solution.py
@@ -80,6 +80,22 @@
     flat = me * mems + core
     first = jnp.minimum(core * part, channels - part)
 
+    def wrap(n, size):
+        return jnp.where(n >= size, n - size, n)
+
+    def for_all(size, action):
+        def body(k, carry):
+            action(k)
+            return carry
+
+        lax.fori_loop(1, size, body, 0)
+
+    def for_devices(action):
+        for m in range(mems):
+            for_all(tiles, lambda k: action(wrap(me + k, tiles), m))
+            if m > 0:
+                action(me, wrap(core + m, mems))
+
     loads = [
         pltpu.make_async_copy(source, target, local_sem.at[i])
         for i, (source, target) in enumerate(
@@ -100,14 +116,10 @@
 
     barrier = pltpu.get_barrier_semaphore()
 
-    def greet(k, carry):
-        other = lax.rem(flat + k, devices)
-        pl.semaphore_signal(
-            barrier, inc=1, device_id=(other // mems, lax.rem(other, mems)), device_id_type=MESH
-        )
-        return carry
-
-    lax.fori_loop(1, devices, greet, 0)
+    def greet(tile, mem):
+        pl.semaphore_signal(barrier, inc=1, device_id=(tile, mem), device_id_type=MESH)
+
+    for_devices(greet)
     for load in loads[4:]:
         load.start()
 
@@ -138,6 +150,22 @@
     for t in range(tiles):
         ask[t] = turned[t : t + 1, :]
 
+    pl.semaphore_wait(barrier, devices - 1)
+
+    def start_ask(k):
+        other = wrap(me + k, tiles)
+        pltpu.make_async_remote_copy(
+            src_ref=ask.at[other],
+            dst_ref=asked.at[me],
+            send_sem=ask_send,
+            recv_sem=ask_recv,
+            device_id=(other, core),
+            device_id_type=MESH,
+        ).start()
+
+    for_all(tiles, start_ask)
+    asked[pl.ds(me, 1)] = ask[pl.ds(me, 1)]
+
     loads[3].wait()
     for b in range(fblocks):
         tall[b * SUB : b * SUB + channels, :] = inc_ref[:, b * LANES : (b + 1) * LANES].astype(f32)
@@ -160,23 +188,6 @@
     spread[...] = jnp.zeros_like(spread)
     for p in range(pairs):
         spread[p, pl.ds(ONES, rows, stride=SUB), :] = jnp.where(live[p], 1.0, 0.0)
-
-    pl.semaphore_wait(barrier, devices - 1)
-
-    def start_ask(k, carry):
-        other = lax.rem(me + k, tiles)
-        pltpu.make_async_remote_copy(
-            src_ref=ask.at[other],
-            dst_ref=asked.at[me],
-            send_sem=ask_send,
-            recv_sem=ask_recv,
-            device_id=(other, core),
-            device_id_type=MESH,
-        ).start()
-        return carry
-
-    lax.fori_loop(1, tiles, start_ask, 0)
-    asked[pl.ds(me, 1)] = ask[pl.ds(me, 1)]
 
     chunk = next(n for n in (512, 384, 256, 128) if cells % n == 0)
     sub = lax.broadcasted_iota(jnp.int32, (SUB, chunk), 0)
@@ -199,9 +210,6 @@
 
         lax.fori_loop(0, cells // chunk, body, 0)
 
-    loads[4].wait()
-    member_stats(prior, 0)
-
     def wait_all(buffer, sem):
         pltpu.make_async_copy(buffer, buffer, sem).wait()
 
@@ -220,8 +228,8 @@
     def rows_of(t):
         return pl.ds(pl.multiple_of(t * slots, slots), slots)
 
-    def start_data(k, carry):
-        other = lax.rem(me + k, tiles)
+    def start_data(k):
+        other = wrap(me + wrap(k - 1 + tiles // 2, tiles - 1) + 1, tiles)
         pltpu.make_async_remote_copy(
             src_ref=served.at[rows_of(other)],
             dst_ref=got.at[rows_of(me)],
@@ -230,16 +238,17 @@
             device_id=(other, core),
             device_id_type=MESH,
         ).start()
-        return carry
-
-    lax.fori_loop(1, tiles, start_data, 0)
+
+    for_all(tiles, start_data)
     got[rows_of(me), :] = served[rows_of(me), :]
 
+    loads[4].wait()
+    member_stats(prior, 0)
     loads[6].wait()
     member_stats(post, 2 * SUB)
 
     def core_copy(buffer, send, recv, k, here):
-        other = lax.rem(core + k, mems)
+        other = wrap(core + k, mems)
         source = here if here is not None else other
         return pltpu.make_async_remote_copy(
             src_ref=buffer.at[core],
@@ -288,23 +297,18 @@
                 value = jnp.where((first + k == c) & (core * part < channels), mine, value)
             spread[p, pl.ds(c, rows, stride=SUB), :] = jnp.where(live[p], value, 0.0)
 
-    group = next(n for n in (12, 8, 4, 3, 2, 1) if rows % n == 0)
-
-    def remap(g, sums):
-        for i in range(group):
-            r = g * group + i
-            here = pl.ds(pl.multiple_of(r * SUB, SUB), SUB)
-            left = jnp.concatenate([spread[p, here, :] for p in range(pairs)], axis=1).astype(bf16)
-            right = jnp.concatenate([weight[r, p] for p in range(pairs)], axis=1)
-            product = lax.dot_general(
-                left, right, (((1,), (1,)), ((), ())), preferred_element_type=f32
-            )
-            value = product / product[ONES : ONES + 1, :]
-            coarse[core, :, pl.ds(pl.multiple_of(r * LANES, LANES), LANES)] = value
-            sums = sums + value * area_ref[pl.ds(r, 1), :]
-        return sums
-
-    sums = lax.fori_loop(0, rows // group, remap, jnp.zeros((SUB, LANES), f32))
+    sums = jnp.zeros((SUB, LANES), f32)
+    for r in range(rows):
+        left = jnp.concatenate(
+            [spread[p, r * SUB : (r + 1) * SUB, :] for p in range(pairs)], axis=1
+        ).astype(bf16)
+        right = jnp.concatenate([weight[r, p] for p in range(pairs)], axis=1)
+        product = lax.dot_general(
+            left, right, (((1,), (1,)), ((), ())), preferred_element_type=f32
+        )
+        value = product / product[ONES : ONES + 1, :]
+        coarse[core, :, r * LANES : (r + 1) * LANES] = value
+        sums = sums + value * area_ref[r : r + 1, :]
 
     for k in range(1, mems):
         core_copy(coarse, coarse_send, coarse_recv, k, core).start()
@@ -314,19 +318,17 @@
     total = jnp.sum(sums, axis=1, keepdims=True)
     level[pl.ds(flat, 1)] = jnp.sum(jnp.where(eye, total, 0.0), axis=0, keepdims=True)[None]
 
-    def start_level(k, carry):
-        other = lax.rem(flat + k, devices)
+    def start_level(tile, mem):
         pltpu.make_async_remote_copy(
             src_ref=level.at[flat],
             dst_ref=level.at[flat],
             send_sem=level_send,
             recv_sem=level_recv,
-            device_id=(other // mems, lax.rem(other, mems)),
+            device_id=(tile, mem),
             device_id_type=MESH,
         ).start()
-        return carry
-
-    lax.fori_loop(1, devices, start_level, 0)
+
+    for_devices(start_level)
     for k in range(1, mems):
         core_copy(coarse, coarse_send, coarse_recv, k, None).wait()
     wait_all(level.at[: devices - 1], level_recv)

time: 24.6 us -> 24.4 us (level)
  no operation moved by 1% of the time
where the time goes in v3:
time: 24.4 us; the launch traced here: 24.2 us
  Pallas kernels  22.6 us (93%)
  other arithmetic  1.58 us (6%)
    pallas_call x1, Pallas kernels, per_device(): pl.pallas_call(functools.partial(kernel, tiles, mems, cap), out_shape=plt...  22.6 us
    convert_element_type x1, other arithmetic, per_device(): return (center + factor * (posterior.astype(f32) - post_mean)).astype(bf16)  1.58 us

profile of v3, /device:TPU:0, one launch (start us, length us, event | category | flops | bytes accessed | tf_op | source)
XLA Modules:
  0.0 24.2 jit_solution(18066927223817068624)
XLA Ops:
  0.0 0.0 copy-start
  0.0 22.6 %remap_and_spread.1 = f32[3,8,3072]{2,1,0:T(8,128)S(1)} custom-call(bf16[6,12288]{1,0:T(8,128)(2,1)} %inc_hbm.1, s32[4,24]{1,0:T(4,128)} %bitcast.11, s32[4,24]{1,0:T(4,128)} %bitcast.12, s32[4,24]{1,0:T(4,128)} %bitcast.13, f32[24,128]{1,0:T(8,128)} %bitcast.10, bf16[24,4,128,128]{3,2,1,0:T(8,128)(2,1)} %weight_hbm.1, bf16[6,40,3072]{2,1,0:T(8,128)(2,1)} %prior_hbm.1, ...), custom_call_target="tpu_custom_call" | custom-call | tf_op jit(solution)/shard_map/remap_and_spread/pallas_call | solution.py:369
  22.7 0.0 copy-done
  22.7 1.6 %add_convert_fusion = bf16[6,40,3072]{2,1,0:T(8,128)(2,1)} fusion(bf16[6,40,3072]{2,1,0:T(8,128)(2,1)S(1)} %copy-done, f32[6,3072]{1,0:T(8,128)S(1)} %get-tuple-element.6, f32[6,3072]{1,0:T(8,128)S(1)} %get-tuple-element.7, f32[6,3072]{1,0:T(8,128)S(1)} %get-tuple-element.5), kind=kLoop, calls=%fused_computation | loop fusion | flops 3686400 | bytes 3170304 | tf_op jit(solution)/shard_map/convert_element_type | solution.py:422
  (1 shorter events, 0.0 us)
Async XLA Ops:
  0.0 22.7 %copy-start = (bf16[6,40,3072]{2,1,0:T(8,128)(2,1)S(1)}, bf16[6,40,3072]{2,1,0:T(8,128)(2,1)}, u32[]{:S(2)}) copy-start(bf16[6,40,3072]{2,1,0:T(8,128)(2,1)} %post_hbm.1) | copy-start | bytes 4423684

commit v4 on v3

--- a/solution.py
+++ b/solution.py
@@ -51,6 +51,8 @@
     served,
     got,
     spread,
+    ratio,
+    shares,
     stats,
     coarse,
     level,
@@ -186,6 +188,7 @@
 
     live = [lane < count[:, p : p + 1] for p in range(pairs)]
     spread[...] = jnp.zeros_like(spread)
+    ratio[...] = jnp.zeros_like(ratio)
     for p in range(pairs):
         spread[p, pl.ds(ONES, rows, stride=SUB), :] = jnp.where(live[p], 1.0, 0.0)
 
@@ -213,6 +216,9 @@
     def wait_all(buffer, sem):
         pltpu.make_async_copy(buffer, buffer, sem).wait()
 
+    loads[4].wait()
+    member_stats(prior, 0)
+
     wait_all(asked.at[: tiles - 1], ask_recv)
     square[...] = jnp.zeros_like(square)
     for t in range(tiles):
@@ -242,8 +248,6 @@
     for_all(tiles, start_data)
     got[rows_of(me), :] = served[rows_of(me), :]
 
-    loads[4].wait()
-    member_stats(prior, 0)
     loads[6].wait()
     member_stats(post, 2 * SUB)
 
@@ -261,6 +265,35 @@
 
     for k in range(1, mems):
         core_copy(stats, stat_send, stat_recv, k, core).start()
+
+    loads[5].wait()
+    loads[7].wait()
+
+    def remap(r):
+        left = jnp.concatenate(
+            [spread[p, r * SUB : (r + 1) * SUB, :] for p in range(pairs)], axis=1
+        ).astype(bf16)
+        right = jnp.concatenate([weight[r, p] for p in range(pairs)], axis=1)
+        return lax.dot_general(
+            left, right, (((1,), (1,)), ((), ())), preferred_element_type=f32
+        )
+
+    for r in range(rows):
+        before[r : r + 1, :] = remap(r)[ONES : ONES + 1, :]
+    rest = area_ref[...] / before[...]
+    for i in range(3):
+        rounded = rest.astype(bf16).astype(f32)
+        ratio[pl.ds(i, rows, stride=SUB), :] = rounded
+        rest = rest - rounded
+    for r in range(rows):
+        right = jnp.concatenate([weight[r, p] for p in range(pairs)], axis=1)
+        share = jnp.dot(
+            ratio[r * SUB : (r + 1) * SUB, :].astype(bf16), right, preferred_element_type=f32
+        )
+        share = jnp.sum(share, axis=0, keepdims=True)
+        for p in range(pairs):
+            shares[p, r : r + 1, :] = share[:, p * LANES : (p + 1) * LANES]
+
     for k in range(1, mems):
         core_copy(stats, stat_send, stat_recv, k, None).wait()
     everyone = members * mems
@@ -284,39 +317,18 @@
         out_ref[1, :, at] = 1.0 + relax_weight * (prior_spread - post_spread) / post_spread
         out_ref[2, :, at] = post_mean
 
-    loads[5].wait()
-    loads[7].wait()
-
     wait_all(got.at[: (tiles - 1) * slots], data_recv)
     picked = jnp.dot(pick[...], got[...], preferred_element_type=f32)
-    for p in range(pairs):
-        for c in range(channels):
-            value = jnp.zeros((rows, LANES), f32)
-            for k in range(part):
-                mine = picked[p * row_pad : p * row_pad + rows, k * LANES : (k + 1) * LANES]
-                value = jnp.where((first + k == c) & (core * part < channels), mine, value)
-            spread[p, pl.ds(c, rows, stride=SUB), :] = jnp.where(live[p], value, 0.0)
-
-    sums = jnp.zeros((SUB, LANES), f32)
-    for r in range(rows):
-        left = jnp.concatenate(
-            [spread[p, r * SUB : (r + 1) * SUB, :] for p in range(pairs)], axis=1
-        ).astype(bf16)
-        right = jnp.concatenate([weight[r, p] for p in range(pairs)], axis=1)
-        product = lax.dot_general(
-            left, right, (((1,), (1,)), ((), ())), preferred_element_type=f32
-        )
-        value = product / product[ONES : ONES + 1, :]
-        coarse[core, :, r * LANES : (r + 1) * LANES] = value
-        sums = sums + value * area_ref[r : r + 1, :]
-
-    for k in range(1, mems):
-        core_copy(coarse, coarse_send, coarse_recv, k, core).start()
-    eye = lax.broadcasted_iota(jnp.int32, (SUB, LANES), 0) == lax.broadcasted_iota(
-        jnp.int32, (SUB, LANES), 1
-    )
-    total = jnp.sum(sums, axis=1, keepdims=True)
-    level[pl.ds(flat, 1)] = jnp.sum(jnp.where(eye, total, 0.0), axis=0, keepdims=True)[None]
+    level_lane = lax.broadcasted_iota(jnp.int32, (1, LANES), 1)
+    row = jnp.where(level_lane == ONES, jnp.sum(area_ref[...], keepdims=True), 0.0)
+    for k in range(part):
+        added = jnp.zeros((rows, LANES), f32)
+        for p in range(pairs):
+            mine = picked[p * row_pad : p * row_pad + rows, k * LANES : (k + 1) * LANES]
+            added = added + jnp.where(live[p], mine * shares[p], 0.0)
+        here = (level_lane == first + k) & (core * part < channels)
+        row = jnp.where(here, jnp.sum(added, keepdims=True), row)
+    level[pl.ds(flat, 1)] = row[None]
 
     def start_level(tile, mem):
         pltpu.make_async_remote_copy(
@@ -329,12 +341,48 @@
         ).start()
 
     for_devices(start_level)
-    for k in range(1, mems):
-        core_copy(coarse, coarse_send, coarse_recv, k, None).wait()
+
+    for p in range(pairs):
+        for c in range(channels):
+            value = jnp.zeros((rows, LANES), f32)
+            for k in range(part):
+                mine = picked[p * row_pad : p * row_pad + rows, k * LANES : (k + 1) * LANES]
+                value = jnp.where((first + k == c) & (core * part < channels), mine, value)
+            spread[p, pl.ds(c, rows, stride=SUB), :] = jnp.where(live[p], value, 0.0)
+
+    pieces = 2
+    piece = rows // pieces
+
+    def coarse_copy(i, k, here):
+        other = wrap(core + k, mems)
+        source = here if here is not None else other
+        at = pl.ds(i * piece * LANES, piece * LANES)
+        return pltpu.make_async_remote_copy(
+            src_ref=coarse.at[core, :, at],
+            dst_ref=coarse.at[source, :, at],
+            send_sem=coarse_send.at[i, other],
+            recv_sem=coarse_recv.at[i, source],
+            device_id=(me, other),
+            device_id_type=MESH,
+        )
+
+    for i in range(pieces):
+        for r in range(i * piece, (i + 1) * piece):
+            product = remap(r)
+            coarse[core, :, r * LANES : (r + 1) * LANES] = product / product[ONES : ONES + 1, :]
+        for k in range(1, mems):
+            coarse_copy(i, k, core).start()
+
+    for i in range(pieces):
+        for k in range(1, mems):
+            coarse_copy(i, k, None).wait()
     wait_all(level.at[: devices - 1], level_recv)
     row = level[0]
     for d in range(1, devices):
         row = row + level[d]
+    eye = lax.broadcasted_iota(jnp.int32, (SUB, LANES), 0) == lax.broadcasted_iota(
+        jnp.int32, (SUB, LANES), 1
+    )
     weighted = jnp.sum(jnp.where(eye, row, 0.0), axis=1, keepdims=True)
     area = weighted[ONES : ONES + 1, :] * (1.0 / mems)
     mean = weighted / area
@@ -389,6 +437,8 @@
             pltpu.VMEM((tiles * slots, part * LANES), bf16),
             pltpu.VMEM((tiles * slots, part * LANES), bf16),
             pltpu.VMEM((pairs, rows * SUB, LANES), f32),
+            pltpu.VMEM((rows * SUB, LANES), f32),
+            pltpu.VMEM((pairs, rows, LANES), f32),
             pltpu.VMEM((mems, 4 * SUB, cells), f32),
             pltpu.VMEM((mems, SUB, cells), f32),
             pltpu.VMEM((devices, 1, LANES), f32),
@@ -399,8 +449,8 @@
             dma,
             dma((mems,)),
             dma((mems,)),
-            dma((mems,)),
-            dma((mems,)),
+            dma((2, mems)),
+            dma((2, mems)),
             dma,
             dma,
         ],

time: 24.4 us -> 23.6 us (0.967)
  Pallas kernels: 22.6 us -> 21.8 us
    pallas_call x1, Pallas kernels: 22.6 us -> 21.8 us  [per_device(): pl.pallas_call(functools.partial(kernel, tiles, mems, cap), out_shape=plt...]
where the time goes in v4:
time: 23.6 us; the launch traced here: 23.4 us
  Pallas kernels  21.8 us (92%)
  other arithmetic  1.58 us (7%)
    pallas_call x1, Pallas kernels, per_device(): pl.pallas_call(functools.partial(kernel, tiles, mems, cap), out_shape=plt...  21.8 us
    convert_element_type x1, other arithmetic, per_device(): return (center + factor * (posterior.astype(f32) - post_mean)).astype(bf16)  1.58 us

profile of v4, /device:TPU:0, one launch (start us, length us, event | category | flops | bytes accessed | tf_op | source)
XLA Modules:
  0.0 23.4 jit_solution(9288837507693512763)
XLA Ops:
  0.0 0.0 copy-start
  0.0 21.8 %remap_and_spread.1 = f32[3,8,3072]{2,1,0:T(8,128)S(1)} custom-call(bf16[6,12288]{1,0:T(8,128)(2,1)} %inc_hbm.1, s32[4,24]{1,0:T(4,128)} %bitcast.11, s32[4,24]{1,0:T(4,128)} %bitcast.12, s32[4,24]{1,0:T(4,128)} %bitcast.13, f32[24,128]{1,0:T(8,128)} %bitcast.10, bf16[24,4,128,128]{3,2,1,0:T(8,128)(2,1)} %weight_hbm.1, bf16[6,40,3072]{2,1,0:T(8,128)(2,1)} %prior_hbm.1, ...), custom_call_target="tpu_custom_call" | custom-call | tf_op jit(solution)/shard_map/remap_and_spread/pallas_call | solution.py:417
  21.8 0.0 copy-done
  21.8 1.6 %add_convert_fusion = bf16[6,40,3072]{2,1,0:T(8,128)(2,1)} fusion(bf16[6,40,3072]{2,1,0:T(8,128)(2,1)S(1)} %copy-done, f32[6,3072]{1,0:T(8,128)S(1)} %get-tuple-element.6, f32[6,3072]{1,0:T(8,128)S(1)} %get-tuple-element.7, f32[6,3072]{1,0:T(8,128)S(1)} %get-tuple-element.5), kind=kLoop, calls=%fused_computation | loop fusion | flops 3686400 | bytes 3170304 | tf_op jit(solution)/shard_map/convert_element_type | solution.py:472
  (1 shorter events, 0.0 us)
Async XLA Ops:
  0.0 21.8 %copy-start = (bf16[6,40,3072]{2,1,0:T(8,128)(2,1)S(1)}, bf16[6,40,3072]{2,1,0:T(8,128)(2,1)}, u32[]{:S(2)}) copy-start(bf16[6,40,3072]{2,1,0:T(8,128)(2,1)} %post_hbm.1) | copy-start | bytes 4423684

commit v5 on v4

--- a/solution.py
+++ b/solution.py
@@ -56,6 +56,7 @@
     stats,
     coarse,
     level,
+    whole,
     local_sem,
     ask_send,
     ask_recv,
@@ -67,6 +68,8 @@
     coarse_recv,
     level_send,
     level_recv,
+    whole_send,
+    whole_recv,
 ):
     channels = inc_ref.shape[0]
     pairs, rows = owner_hbm.shape
@@ -76,10 +79,8 @@
     slots = got.shape[0] // tiles
     row_pad = pick.shape[0] // pairs
     members, cells = prior.shape[1], prior.shape[2]
-    devices = tiles * mems
     me = lax.axis_index("tile")
     core = lax.axis_index("mem")
-    flat = me * mems + core
     first = jnp.minimum(core * part, channels - part)
 
     def wrap(n, size):
@@ -91,12 +92,6 @@
             return carry
 
         lax.fori_loop(1, size, body, 0)
-
-    def for_devices(action):
-        for m in range(mems):
-            for_all(tiles, lambda k: action(wrap(me + k, tiles), m))
-            if m > 0:
-                action(me, wrap(core + m, mems))
 
     loads = [
         pltpu.make_async_copy(source, target, local_sem.at[i])
@@ -121,7 +116,9 @@
     def greet(tile, mem):
         pl.semaphore_signal(barrier, inc=1, device_id=(tile, mem), device_id_type=MESH)
 
-    for_devices(greet)
+    for_all(tiles, lambda k: greet(wrap(me + k, tiles), core))
+    for k in range(1, mems):
+        greet(me, wrap(core + k, mems))
     for load in loads[4:]:
         load.start()
 
@@ -152,7 +149,7 @@
     for t in range(tiles):
         ask[t] = turned[t : t + 1, :]
 
-    pl.semaphore_wait(barrier, devices - 1)
+    pl.semaphore_wait(barrier, tiles + mems - 2)
 
     def start_ask(k):
         other = wrap(me + k, tiles)
@@ -328,19 +325,19 @@
             added = added + jnp.where(live[p], mine * shares[p], 0.0)
         here = (level_lane == first + k) & (core * part < channels)
         row = jnp.where(here, jnp.sum(added, keepdims=True), row)
-    level[pl.ds(flat, 1)] = row[None]
-
-    def start_level(tile, mem):
+    level[pl.ds(me, 1)] = row[None]
+
+    def start_level(k):
         pltpu.make_async_remote_copy(
-            src_ref=level.at[flat],
-            dst_ref=level.at[flat],
+            src_ref=level.at[me],
+            dst_ref=level.at[me],
             send_sem=level_send,
             recv_sem=level_recv,
-            device_id=(tile, mem),
+            device_id=(wrap(me + k, tiles), core),
             device_id_type=MESH,
         ).start()
 
-    for_devices(start_level)
+    for_all(tiles, start_level)
 
     for p in range(pairs):
         for c in range(channels):
@@ -373,13 +370,21 @@
         for k in range(1, mems):
             coarse_copy(i, k, core).start()
 
+    wait_all(level.at[: tiles - 1], level_recv)
+    row = level[0]
+    for t in range(1, tiles):
+        row = row + level[t]
+    whole[pl.ds(core, 1)] = row[None]
+    for k in range(1, mems):
+        core_copy(whole, whole_send, whole_recv, k, core).start()
     for i in range(pieces):
         for k in range(1, mems):
             coarse_copy(i, k, None).wait()
-    wait_all(level.at[: devices - 1], level_recv)
-    row = level[0]
-    for d in range(1, devices):
-        row = row + level[d]
+    for k in range(1, mems):
+        core_copy(whole, whole_send, whole_recv, k, None).wait()
+    row = whole[0]
+    for m in range(1, mems):
+        row = row + whole[m]
     eye = lax.broadcasted_iota(jnp.int32, (SUB, LANES), 0) == lax.broadcasted_iota(
         jnp.int32, (SUB, LANES), 1
     )
@@ -392,7 +397,7 @@
         out_ref[0, :, at] = out_ref[0, :, at] + (value - mean)
     wait_all(asked.at[: tiles - 1], ask_send)
     wait_all(got.at[: (tiles - 1) * slots], data_send)
-    wait_all(level.at[: devices - 1], level_send)
+    wait_all(level.at[: tiles - 1], level_send)
 
 
 def per_device(
@@ -410,7 +415,6 @@
     part = -(-channels // mems)
     fine_pad = round_up(fblocks, LANES)
     row_pad = round_up(rows, 16)
-    devices = tiles * mems
     vmem = pl.BlockSpec(memory_space=pltpu.VMEM)
     hbm = pl.BlockSpec(memory_space=pltpu.HBM)
     dma = pltpu.SemaphoreType.DMA
@@ -441,7 +445,8 @@
             pltpu.VMEM((pairs, rows, LANES), f32),
             pltpu.VMEM((mems, 4 * SUB, cells), f32),
             pltpu.VMEM((mems, SUB, cells), f32),
-            pltpu.VMEM((devices, 1, LANES), f32),
+            pltpu.VMEM((tiles, 1, LANES), f32),
+            pltpu.VMEM((mems, 1, LANES), f32),
             dma((8,)),
             dma,
             dma,
@@ -453,6 +458,8 @@
             dma((2, mems)),
             dma,
             dma,
+            dma((mems,)),
+            dma((mems,)),
         ],
         compiler_params=pltpu.CompilerParams(
             collective_id=0, has_side_effects=True, vmem_limit_bytes=56 * 1024 * 1024

time: 23.6 us -> 23.7 us (level)
  no operation moved by 1% of the time
where the time goes in v5:
time: 23.7 us; the launch traced here: 23.5 us
  Pallas kernels  21.9 us (92%)
  other arithmetic  1.58 us (7%)
    pallas_call x1, Pallas kernels, per_device(): pl.pallas_call(functools.partial(kernel, tiles, mems, cap), out_shape=plt...  21.9 us
    convert_element_type x1, other arithmetic, per_device(): return (center + factor * (posterior.astype(f32) - post_mean)).astype(bf16)  1.58 us

profile of v5, /device:TPU:0, one launch (start us, length us, event | category | flops | bytes accessed | tf_op | source)
XLA Modules:
  0.0 23.5 jit_solution(1227619311638914819)
XLA Ops:
  0.0 0.0 copy-start
  0.0 21.9 %remap_and_spread.1 = f32[3,8,3072]{2,1,0:T(8,128)S(1)} custom-call(bf16[6,12288]{1,0:T(8,128)(2,1)} %inc_hbm.1, s32[4,24]{1,0:T(4,128)} %bitcast.11, s32[4,24]{1,0:T(4,128)} %bitcast.12, s32[4,24]{1,0:T(4,128)} %bitcast.13, f32[24,128]{1,0:T(8,128)} %bitcast.10, bf16[24,4,128,128]{3,2,1,0:T(8,128)(2,1)} %weight_hbm.1, bf16[6,40,3072]{2,1,0:T(8,128)(2,1)} %prior_hbm.1, ...), custom_call_target="tpu_custom_call" | custom-call | tf_op jit(solution)/shard_map/remap_and_spread/pallas_call | solution.py:421
  21.9 0.0 copy-done
  22.0 1.6 %add_convert_fusion = bf16[6,40,3072]{2,1,0:T(8,128)(2,1)} fusion(bf16[6,40,3072]{2,1,0:T(8,128)(2,1)S(1)} %copy-done, f32[6,3072]{1,0:T(8,128)S(1)} %get-tuple-element.6, f32[6,3072]{1,0:T(8,128)S(1)} %get-tuple-element.7, f32[6,3072]{1,0:T(8,128)S(1)} %get-tuple-element.5), kind=kLoop, calls=%fused_computation | loop fusion | flops 3686400 | bytes 3170304 | tf_op jit(solution)/shard_map/convert_element_type | solution.py:479
  (1 shorter events, 0.0 us)
Async XLA Ops:
  0.0 21.9 %copy-start = (bf16[6,40,3072]{2,1,0:T(8,128)(2,1)S(1)}, bf16[6,40,3072]{2,1,0:T(8,128)(2,1)}, u32[]{:S(2)}) copy-start(bf16[6,40,3072]{2,1,0:T(8,128)(2,1)} %post_hbm.1) | copy-start | bytes 4423684

commit v6 on v5

--- a/solution.py
+++ b/solution.py
@@ -70,6 +70,8 @@
     level_recv,
     whole_send,
     whole_recv,
+    share_send,
+    share_recv,
 ):
     channels = inc_ref.shape[0]
     pairs, rows = owner_hbm.shape
@@ -266,30 +268,39 @@
     loads[5].wait()
     loads[7].wait()
 
+    def rows_at(r):
+        return pl.ds(r * SUB if isinstance(r, int) else pl.multiple_of(r * SUB, SUB), SUB)
+
     def remap(r):
         left = jnp.concatenate(
-            [spread[p, r * SUB : (r + 1) * SUB, :] for p in range(pairs)], axis=1
+            [spread[p, rows_at(r), :] for p in range(pairs)], axis=1
         ).astype(bf16)
         right = jnp.concatenate([weight[r, p] for p in range(pairs)], axis=1)
         return lax.dot_general(
             left, right, (((1,), (1,)), ((), ())), preferred_element_type=f32
         )
 
-    for r in range(rows):
-        before[r : r + 1, :] = remap(r)[ONES : ONES + 1, :]
+    own_rows = rows // mems
+    before[...] = jnp.ones_like(before)
+    shares[core] = jnp.zeros(shares.shape[1:], f32)
+    for i in range(own_rows):
+        r = core * own_rows + i
+        before[pl.ds(r, 1), :] = remap(r)[ONES : ONES + 1, :]
     rest = area_ref[...] / before[...]
     for i in range(3):
         rounded = rest.astype(bf16).astype(f32)
         ratio[pl.ds(i, rows, stride=SUB), :] = rounded
         rest = rest - rounded
-    for r in range(rows):
+    for i in range(own_rows):
+        r = core * own_rows + i
         right = jnp.concatenate([weight[r, p] for p in range(pairs)], axis=1)
-        share = jnp.dot(
-            ratio[r * SUB : (r + 1) * SUB, :].astype(bf16), right, preferred_element_type=f32
-        )
+        left = ratio[pl.ds(pl.multiple_of(r * SUB, SUB), SUB), :].astype(bf16)
+        share = jnp.dot(left, right, preferred_element_type=f32)
         share = jnp.sum(share, axis=0, keepdims=True)
         for p in range(pairs):
-            shares[p, r : r + 1, :] = share[:, p * LANES : (p + 1) * LANES]
+            shares[core, p, i : i + 1, :] = share[:, p * LANES : (p + 1) * LANES]
+    for k in range(1, mems):
+        core_copy(shares, share_send, share_recv, k, core).start()
 
     for k in range(1, mems):
         core_copy(stats, stat_send, stat_recv, k, None).wait()
@@ -314,6 +325,13 @@
         out_ref[1, :, at] = 1.0 + relax_weight * (prior_spread - post_spread) / post_spread
         out_ref[2, :, at] = post_mean
 
+    for k in range(1, mems):
+        core_copy(shares, share_send, share_recv, k, None).wait()
+    every = [
+        jnp.concatenate([shares[m, p, :own_rows, :] for m in range(mems)], axis=0)
+        for p in range(pairs)
+    ]
+
     wait_all(got.at[: (tiles - 1) * slots], data_recv)
     picked = jnp.dot(pick[...], got[...], preferred_element_type=f32)
     level_lane = lax.broadcasted_iota(jnp.int32, (1, LANES), 1)
@@ -322,7 +340,7 @@
         added = jnp.zeros((rows, LANES), f32)
         for p in range(pairs):
             mine = picked[p * row_pad : p * row_pad + rows, k * LANES : (k + 1) * LANES]
-            added = added + jnp.where(live[p], mine * shares[p], 0.0)
+            added = added + jnp.where(live[p], mine * every[p], 0.0)
         here = (level_lane == first + k) & (core * part < channels)
         row = jnp.where(here, jnp.sum(added, keepdims=True), row)
     level[pl.ds(me, 1)] = row[None]
@@ -442,7 +460,7 @@
             pltpu.VMEM((tiles * slots, part * LANES), bf16),
             pltpu.VMEM((pairs, rows * SUB, LANES), f32),
             pltpu.VMEM((rows * SUB, LANES), f32),
-            pltpu.VMEM((pairs, rows, LANES), f32),
+            pltpu.VMEM((mems, pairs, round_up(rows // mems, SUB), LANES), f32),
             pltpu.VMEM((mems, 4 * SUB, cells), f32),
             pltpu.VMEM((mems, SUB, cells), f32),
             pltpu.VMEM((tiles, 1, LANES), f32),
@@ -458,6 +476,8 @@
             dma((2, mems)),
             dma,
             dma,
+            dma((mems,)),
+            dma((mems,)),
             dma((mems,)),
             dma((mems,)),
         ],

time: 23.7 us -> 23.7 us (level)
  no operation moved by 1% of the time
where the time goes in v6:
time: 23.7 us; the launch traced here: 23.6 us
  Pallas kernels  21.9 us (92%)
  other arithmetic  1.58 us (7%)
    pallas_call x1, Pallas kernels, per_device(): pl.pallas_call(functools.partial(kernel, tiles, mems, cap), out_shape=plt...  21.9 us
    convert_element_type x1, other arithmetic, per_device(): return (center + factor * (posterior.astype(f32) - post_mean)).astype(bf16)  1.58 us

profile of v6, /device:TPU:0, one launch (start us, length us, event | category | flops | bytes accessed | tf_op | source)
XLA Modules:
  0.0 23.6 jit_solution(3705230236022495542)
XLA Ops:
  0.0 0.0 copy-start
  0.0 21.9 %remap_and_spread.1 = f32[3,8,3072]{2,1,0:T(8,128)S(1)} custom-call(bf16[6,12288]{1,0:T(8,128)(2,1)} %inc_hbm.1, s32[4,24]{1,0:T(4,128)} %bitcast.11, s32[4,24]{1,0:T(4,128)} %bitcast.12, s32[4,24]{1,0:T(4,128)} %bitcast.13, f32[24,128]{1,0:T(8,128)} %bitcast.10, bf16[24,4,128,128]{3,2,1,0:T(8,128)(2,1)} %weight_hbm.1, bf16[6,40,3072]{2,1,0:T(8,128)(2,1)} %prior_hbm.1, ...), custom_call_target="tpu_custom_call" | custom-call | tf_op jit(solution)/shard_map/remap_and_spread/pallas_call | solution.py:439
  22.0 0.0 copy-done
  22.0 1.6 %add_convert_fusion = bf16[6,40,3072]{2,1,0:T(8,128)(2,1)} fusion(bf16[6,40,3072]{2,1,0:T(8,128)(2,1)S(1)} %copy-done, f32[6,3072]{1,0:T(8,128)S(1)} %get-tuple-element.6, f32[6,3072]{1,0:T(8,128)S(1)} %get-tuple-element.7, f32[6,3072]{1,0:T(8,128)S(1)} %get-tuple-element.5), kind=kLoop, calls=%fused_computation | loop fusion | flops 3686400 | bytes 3170304 | tf_op jit(solution)/shard_map/convert_element_type | solution.py:499
  (1 shorter events, 0.0 us)
Async XLA Ops:
  0.0 22.0 %copy-start = (bf16[6,40,3072]{2,1,0:T(8,128)(2,1)S(1)}, bf16[6,40,3072]{2,1,0:T(8,128)(2,1)}, u32[]{:S(2)}) copy-start(bf16[6,40,3072]{2,1,0:T(8,128)(2,1)} %post_hbm.1) | copy-start | bytes 4423684

commit v7 on v5

--- a/solution.py
+++ b/solution.py
@@ -232,7 +232,7 @@
         return pl.ds(pl.multiple_of(t * slots, slots), slots)
 
     def start_data(k):
-        other = wrap(me + wrap(k - 1 + tiles // 2, tiles - 1) + 1, tiles)
+        other = wrap(me + k, tiles)
         pltpu.make_async_remote_copy(
             src_ref=served.at[rows_of(other)],
             dst_ref=got.at[rows_of(me)],

time: 23.7 us -> 23.9 us (level)
  no operation moved by 1% of the time
where the time goes in v7:
time: 23.9 us; the launch traced here: 23.8 us
  Pallas kernels  22.1 us (92%)
  other arithmetic  1.58 us (7%)
    pallas_call x1, Pallas kernels, per_device(): pl.pallas_call(functools.partial(kernel, tiles, mems, cap), out_shape=plt...  22.1 us
    convert_element_type x1, other arithmetic, per_device(): return (center + factor * (posterior.astype(f32) - post_mean)).astype(bf16)  1.58 us

profile of v7, /device:TPU:0, one launch (start us, length us, event | category | flops | bytes accessed | tf_op | source)
XLA Modules:
  0.0 23.8 jit_solution(219427749084922071)
XLA Ops:
  0.0 0.0 copy-start
  0.0 22.1 %remap_and_spread.1 = f32[3,8,3072]{2,1,0:T(8,128)S(1)} custom-call(bf16[6,12288]{1,0:T(8,128)(2,1)} %inc_hbm.1, s32[4,24]{1,0:T(4,128)} %bitcast.11, s32[4,24]{1,0:T(4,128)} %bitcast.12, s32[4,24]{1,0:T(4,128)} %bitcast.13, f32[24,128]{1,0:T(8,128)} %bitcast.10, bf16[24,4,128,128]{3,2,1,0:T(8,128)(2,1)} %weight_hbm.1, bf16[6,40,3072]{2,1,0:T(8,128)(2,1)} %prior_hbm.1, ...), custom_call_target="tpu_custom_call" | custom-call | tf_op jit(solution)/shard_map/remap_and_spread/pallas_call | solution.py:421
  22.2 0.0 copy-done
  22.2 1.6 %add_convert_fusion = bf16[6,40,3072]{2,1,0:T(8,128)(2,1)} fusion(bf16[6,40,3072]{2,1,0:T(8,128)(2,1)S(1)} %copy-done, f32[6,3072]{1,0:T(8,128)S(1)} %get-tuple-element.6, f32[6,3072]{1,0:T(8,128)S(1)} %get-tuple-element.7, f32[6,3072]{1,0:T(8,128)S(1)} %get-tuple-element.5), kind=kLoop, calls=%fused_computation | loop fusion | flops 3686400 | bytes 3170304 | tf_op jit(solution)/shard_map/convert_element_type | solution.py:479
  (1 shorter events, 0.0 us)
Async XLA Ops:
  0.0 22.2 %copy-start = (bf16[6,40,3072]{2,1,0:T(8,128)(2,1)S(1)}, bf16[6,40,3072]{2,1,0:T(8,128)(2,1)}, u32[]{:S(2)}) copy-start(bf16[6,40,3072]{2,1,0:T(8,128)(2,1)} %post_hbm.1) | copy-start | bytes 4423684
